TPU v7x, 32 devices: a whole 2x2x4 slice. The times are simulated.
32 devices in a mesh: cable: 2 (over y), chan: 4 (over z), seg: 2 (over x), freq: 2 (over core).
Axes of the slice: x: 2, y: 2, z: 4, core: 2. Of those that a mesh axis runs over, the one named last changes fastest.
Arguments:
- samples: bfloat16 [512, 16, 8192], P(('cable', 'chan'), 'seg'), parts along dimension 0, may hold values from -24 to 24
- live: int32 [512, 16], P('cable'), parts along dimension 0, may hold values from 0 to 1, as said below
Outputs:
- stack: bfloat16 [512, 64, 2, 256], P(('cable', 'chan', 'seg'), None, None, 'freq'), parts along dimension 0
There are 2 independent parts, one for each index of `cable`. A program takes and returns all parts, laid end to end along the dimension named above; each array names one. Nothing has to cross between parts.
Inputs may be any that keep to these rules, and one draw needn't show every extreme that they name: `live`: 1 marks a usable segment of a channel and 0 an unusable one; in every draw some channels are 0 in every segment.
All inputs are finite; a program needn't handle non-finite values.
Results may differ from a plain program's by a relative error of at most 0.006.
Values may be sent and summed in bfloat16 or wider, within the bound.
A program may use at most 64 MiB of HBM per device.

v0:
```python
import functools
import math

import jax
import jax.numpy as jnp
from jax import lax
from jax.experimental import pallas as pl
from jax.experimental.pallas import tpu as pltpu
from jax.sharding import PartitionSpec as P

BINS = 256
OFFSETS = 64
EPSILON = 1e-06
QUARTERS = 4
FINE = 64
CHUNK_CH = 8
KB = 16
MESH = pl.DeviceIdType.MESH


def unit_circle(first, step, count, length):
    t = first + step * lax.broadcasted_iota(jnp.int32, (count, BINS), 0)
    k = 1 + lax.broadcasted_iota(jnp.int32, (count, BINS), 1)
    m = lax.rem(t * k, length)
    m = jnp.where(m >= length // 2, m - length, m)
    y = m.astype(jnp.float32) * (math.pi / length)
    y2 = y * y
    sine = jnp.full_like(y, 1.0 / math.factorial(13))
    for order in (11, 9, 7, 5, 3, 1):
        sine = sine * y2 + (-1.0) ** (order // 2) / math.factorial(order)
    sine = sine * y
    cosine = jnp.full_like(y, -1.0 / math.factorial(14))
    for order in (12, 10, 8, 6, 4, 2, 0):
        cosine = cosine * y2 + (-1.0) ** (order // 2) / math.factorial(order)
    return 1.0 - 2.0 * sine * sine, 2.0 * sine * cosine


def kernel(
    n_chan, n_seg, n_freq, samples, live_hbm, out, live_in, live, xs, tab, seeds, snd, win, merged, lv, inv,
    live_sem, x_sem, send_sem, recv_sem, along_sem, across_sem,
    side, side_recv, side_send,
):
    length = samples.shape[1]
    quarter = length // QUARTERS
    total_segs, chans = live_in.shape
    ch_dev = chans // n_chan
    segs = samples.shape[0] // ch_dev
    owned = ch_dev // n_seg
    half = BINS // n_freq
    core_ch = ch_dev // n_freq
    gpc = n_seg // n_freq
    chunk_rows = CHUNK_CH * segs
    chunks = core_ch // CHUNK_CH
    per_granule = owned // CHUNK_CH
    z, x, c = lax.axis_index("chan"), lax.axis_index("seg"), lax.axis_index("freq")

    def fetch(b, q):
        row = pl.multiple_of((c * chunks + b) * chunk_rows, chunk_rows)
        return pltpu.make_async_copy(
            samples.at[pl.ds(row, chunk_rows), pl.ds(q * quarter, quarter)],
            xs.at[b, pl.ds(q * chunk_rows, chunk_rows), :],
            x_sem.at[b, q],
        )

    for b in range(chunks):
        for q in range(QUARTERS):
            fetch(b, q).start()
    live_copy = pltpu.make_async_copy(live_hbm, live_in, live_sem)
    live_copy.start()

    barrier = pltpu.get_barrier_semaphore()
    for dz in (-1, 0, 1):
        near = jnp.logical_and(z + dz >= 0, z + dz < n_chan)
        for tx in range(n_seg):
            for tc in range(n_freq):
                other = near if dz else jnp.logical_or(x != tx, c != tc)

                @pl.when(other)
                def _():
                    pl.semaphore_signal(
                        barrier, inc=1, device_id={"chan": z + dz, "seg": tx, "freq": tc},
                        device_id_type=MESH,
                    )

    fine_cos, fine_sin = unit_circle(0, 1, FINE, length)
    coarse_cos, coarse_sin = unit_circle(0, FINE, quarter // FINE, length)
    seeds[0] = coarse_cos
    seeds[1] = coarse_sin

    def table_rows(a, _):
        ca, sa = seeds[0, pl.ds(a, 1), :], seeds[1, pl.ds(a, 1), :]
        rows = pl.ds(pl.multiple_of(a * FINE, FINE), FINE)
        tab[rows, :BINS] = (ca * fine_cos - sa * fine_sin).astype(jnp.bfloat16)
        tab[rows, BINS:] = (-(sa * fine_cos + ca * fine_sin)).astype(jnp.bfloat16)
        return 0

    lax.fori_loop(0, quarter // FINE, table_rows, 0, unroll=4)

    live_copy.wait()
    live[...] = live_in[...].astype(jnp.float32).T
    degree = n_seg * n_freq
    up = (z > 0).astype(jnp.int32)
    down = (z < n_chan - 1).astype(jnp.int32)
    pl.semaphore_wait(barrier, degree - 1 + degree * (up + down))

    def descriptor(b, w, h):
        bb, part = b // per_granule, b % per_granule
        granule = c * gpc + bb
        below = (granule < w).astype(jnp.int32)
        tz, tx = z - below, granule - w + below * n_seg
        rows = pl.ds(pl.multiple_of(b * chunk_rows, chunk_rows), chunk_rows)
        dst_rows = pl.ds(pl.multiple_of(part * chunk_rows, chunk_rows), chunk_rows)
        src = snd.at[h, rows, :]
        dst = win.at[x, w, dst_rows, :]
        remote = pltpu.make_async_remote_copy(
            src_ref=src, dst_ref=dst, send_sem=send_sem.at[b, w, h], recv_sem=recv_sem.at[x, w, part],
            device_id={"chan": tz, "seg": tx, "freq": jnp.int32(h)}, device_id_type=MESH,
        )
        local = pltpu.make_async_copy(src, dst, recv_sem.at[x, w, part])
        mine = jnp.logical_and(jnp.logical_and(tz == z, tx == x), c == h)
        straight = jnp.logical_or(below == 0, jnp.logical_and(tz >= 0, tx == x))
        return remote, local, mine, jnp.logical_and(straight, jnp.logical_not(mine))

    half_way = per_granule // 2 if n_seg == 2 and n_freq == 2 else per_granule

    def detour(b, h):
        part = b % per_granule
        rows = pl.ds(pl.multiple_of(b * chunk_rows, chunk_rows), chunk_rows)
        slot = jnp.maximum(part - half_way, 0)
        copy = pltpu.make_async_remote_copy(
            src_ref=snd.at[h, rows, :], dst_ref=side.at[slot], send_sem=send_sem.at[b, n_seg, h],
            recv_sem=side_recv.at[slot],
            device_id={"chan": z - 1, "seg": x, "freq": jnp.int32(h)}, device_id_type=MESH,
        )
        last = c * gpc + b // per_granule == n_seg - 1
        used = jnp.logical_and(jnp.logical_and(z > 0, x == 0), jnp.logical_and(last, part >= half_way))
        return copy, used

    def onward(slot):
        rows = pl.ds((half_way + slot) * chunk_rows, chunk_rows)
        copy = pltpu.make_async_remote_copy(
            src_ref=side.at[slot], dst_ref=win.at[0, n_seg, rows, :], send_sem=side_send.at[slot],
            recv_sem=recv_sem.at[0, n_seg, half_way + slot],
            device_id={"chan": z, "seg": jnp.int32(n_seg - 1), "freq": c}, device_id_type=MESH,
        )
        return copy, jnp.logical_and(z < n_chan - 1, x == 0)

    def along_used(sx, part):
        used = jnp.logical_and(z > 0, sx != x)
        if part >= half_way and sx == 0:
            used = jnp.logical_and(used, x != n_seg - 1)
        return used

    def arrived(sx, w, part):
        dst = win.at[sx, w, pl.ds(part * chunk_rows, chunk_rows), :]
        pltpu.make_async_copy(dst, dst, recv_sem.at[sx, w, part]).wait()

    def relay(sx, w, part, to_w, tz, tx, sem):
        rows = pl.ds(part * chunk_rows, chunk_rows)
        return pltpu.make_async_remote_copy(
            src_ref=win.at[sx, w, rows, :], dst_ref=win.at[sx, to_w, rows, :], send_sem=sem,
            recv_sem=recv_sem.at[sx, to_w, part],
            device_id={"chan": tz, "seg": tx, "freq": c}, device_id_type=MESH,
        )

    def along(sx, part):
        return relay(sx, 0, part, n_seg, z - 1, x, along_sem.at[sx, part])

    def across(sx, w, tx, part):
        return relay(sx, w, part, w + x - tx, z, jnp.int32(tx), across_sem.at[sx, w - 1, tx, part])

    has_above = z < n_chan - 1

    def is_hub(sx, w):
        granule = x + w - n_seg
        own = jnp.logical_and(sx == x, jnp.logical_and(granule >= 0, granule < n_seg - 1))
        own = jnp.logical_and(own, jnp.logical_or(granule < n_seg - 2, x < n_seg - 1))
        first = jnp.logical_and(w == n_seg, jnp.logical_and(sx < x, x < n_seg - 1))
        return jnp.logical_and(has_above, jnp.logical_or(own, first))

    def hub_target(sx, w, tx):
        return jnp.logical_and(is_hub(sx, w), jnp.logical_and(tx > x + w - n_seg, tx != x))

    lane_k = 1 + lax.broadcasted_iota(jnp.int32, (1, BINS), 1)
    phase = lane_k % 4
    alpha = jnp.where(phase == 0, 1.0, jnp.where(phase == 2, -1.0, 0.0))
    beta = jnp.where(phase == 1, 1.0, jnp.where(phase == 3, -1.0, 0.0))
    sigma = jnp.where(lane_k % 2 == 0, 1.0, -1.0)

    def transform(b, _):
        for q in range(QUARTERS):
            fetch(b, q).wait()
        acc = jnp.dot(xs[b], tab[...], preferred_element_type=jnp.float32)
        part = [acc[q * chunk_rows : (q + 1) * chunk_rows] for q in range(QUARTERS)]
        re = [p[:, :BINS] for p in part]
        im = [p[:, BINS:] for p in part]
        odd_re, odd_im = re[1] + sigma * re[3], im[1] + sigma * im[3]
        full_re = re[0] + sigma * re[2] + (alpha * odd_re + beta * odd_im)
        full_im = im[0] + sigma * im[2] + (alpha * odd_im - beta * odd_re)
        energy = jnp.sum(full_re * full_re + full_im * full_im, axis=1, keepdims=True)
        scaling = lax.rsqrt(energy / (2 * BINS) + EPSILON)
        first = pl.multiple_of(z * ch_dev + c * core_ch + b * CHUNK_CH, CHUNK_CH)
        usable = live[pl.ds(first, CHUNK_CH), :]
        usable = jnp.broadcast_to(usable[:, None, :], (CHUNK_CH, segs, total_segs))
        column = lax.broadcasted_iota(jnp.int32, usable.shape, 2)
        segment = x * segs + lax.broadcasted_iota(jnp.int32, usable.shape, 1)
        usable = jnp.where(column == segment, usable, 0.0).reshape(chunk_rows, total_segs)
        usable = jnp.sum(usable, axis=1, keepdims=True)
        white_re = (full_re * scaling * usable).astype(jnp.bfloat16)
        white_im = (full_im * scaling * usable).astype(jnp.bfloat16)
        rows = pl.ds(pl.multiple_of(b * chunk_rows, chunk_rows), chunk_rows)
        for h in range(n_freq):
            snd[h, rows, :half] = white_re[:, h * half : (h + 1) * half]
            snd[h, rows, half:] = white_im[:, h * half : (h + 1) * half]
        for w in range(n_seg, -1, -1):
            for h in range(n_freq):
                remote, local, mine, other = descriptor(b, w, h)
                pl.when(other)(remote.start)
                pl.when(mine)(local.start)
        if half_way < per_granule:
            for h in range(n_freq):
                copy, used = detour(b, h)
                pl.when(used)(copy.start)
        return 0

    lax.fori_loop(0, chunks, transform, 0)

    last_block = chans // owned - 1
    for w in range(n_seg + 1):
        block = z * n_seg + x + w
        row = pl.multiple_of(jnp.minimum(block, last_block) * owned, owned)
        rows = live[pl.ds(row, owned), :]
        lv[w * owned : (w + 1) * owned, :] = jnp.where(block <= last_block, rows, 0.0)
    twice = (
        lax.broadcasted_iota(jnp.int32, (2 * OFFSETS, OFFSETS), 0) // 2
        == lax.broadcasted_iota(jnp.int32, (2 * OFFSETS, OFFSETS), 1)
    ).astype(jnp.float32).astype(jnp.bfloat16)
    ones = jnp.ones((total_segs, half), jnp.bfloat16)

    def count_pairs(i, _):
        both = (lv[pl.ds(i, OFFSETS), :] * lv[pl.ds(i, 1), :]).astype(jnp.bfloat16)
        both = jnp.dot(twice, both, preferred_element_type=jnp.float32).astype(jnp.bfloat16)
        pairs = jnp.dot(both, ones, preferred_element_type=jnp.float32)
        pairs = jnp.maximum(pairs, 1.0)
        guess = pl.reciprocal(pairs, approx=True)
        inv[i] = guess * (2.0 - pairs * guess)
        return 0

    for part in range(per_granule):
        lax.fori_loop(part * CHUNK_CH, (part + 1) * CHUNK_CH, count_pairs, 0, unroll=CHUNK_CH)
        for w in range(n_seg, 0, -1):
            for sx in range(n_seg):

                @pl.when(is_hub(sx, w))
                def _():
                    arrived(sx, w, part)
                    for tx in range(n_seg):
                        pl.when(hub_target(sx, w, tx))(across(sx, w, tx, part).start)

        for sx in range(n_seg):
            arrived(sx, 0, part)
            pl.when(along_used(sx, part))(along(sx, part).start)

        if part >= half_way:
            copy, used = onward(part - half_way)

            @pl.when(used)
            def _():
                place = side.at[part - half_way]
                pltpu.make_async_copy(place, place, side_recv.at[part - half_way]).wait()
                copy.start()

    span = n_seg * segs
    row_id = lax.broadcasted_iota(jnp.int32, (2 * KB, KB * span), 0)
    col_id = lax.broadcasted_iota(jnp.int32, (2 * KB, KB * span), 1) // span
    hit = row_id // 2 == col_id
    sum_re = jnp.where(jnp.logical_and(hit, row_id % 2 == 0), 1.0, 0.0).astype(jnp.bfloat16)
    sum_im = jnp.where(jnp.logical_and(hit, row_id % 2 == 1), 1.0, 0.0).astype(jnp.bfloat16)

    sub_parts = KB // CHUNK_CH
    for t in range((n_seg + 1) * owned // KB):
        w, place = divmod(t * KB, owned)
        inside = z + (x + w) // n_seg < n_chan

        @pl.when(inside)
        def _():
            for sx in range(n_seg):
                for part in range(place // CHUNK_CH, place // CHUNK_CH + sub_parts):
                    if w > 0:
                        pl.when(jnp.logical_not(is_hub(sx, w)))(functools.partial(arrived, sx, w, part))

            def merge(m, _):
                rows = pl.ds(pl.multiple_of((place + 2 * m) * segs, 2 * segs), 2 * segs)
                parts = [win[sx, w, rows, :].astype(jnp.float32) for sx in range(n_seg)]
                for e in range(2):
                    whole = jnp.concatenate([p[e * segs : (e + 1) * segs] for p in parts], axis=0)
                    merged[t * KB + 2 * m + e] = whole.astype(jnp.bfloat16)
                return 0

            lax.fori_loop(0, KB // 2, merge, 0, unroll=4)

        @pl.when(jnp.logical_not(inside))
        def _():
            merged[t * KB : (t + 1) * KB] = jnp.zeros((KB,) + merged.shape[1:], jnp.bfloat16)

        groups = [a for a in range(owned // KB) if 0 <= t - 1 - a < OFFSETS // KB]

        def correlate(n, _):
            group = groups[0] + n // KB
            i = groups[0] * KB + n
            kb = t - 1 - group
            own = merged[i]
            other = merged[pl.ds(i + KB * kb, KB)]
            own_re, own_im = own[None, :, :half], own[None, :, half:]
            other_re, other_im = other[:, :, :half], other[:, :, half:]
            re = own_re * other_re + own_im * other_im
            im = own_re * other_im - own_im * other_re
            total = jnp.dot(
                sum_re, re.reshape(KB * span, half), preferred_element_type=jnp.float32
            ) + jnp.dot(sum_im, im.reshape(KB * span, half), preferred_element_type=jnp.float32)
            rows = pl.ds(pl.multiple_of(2 * KB * kb, 2 * KB), 2 * KB)
            out[i, rows, :] = (total * inv[i, rows, :]).astype(jnp.bfloat16)
            return 0

        if groups:
            lax.fori_loop(0, len(groups) * KB, correlate, 0, unroll=16)

    def drain(b, _):
        for w in range(n_seg + 1):
            for h in range(n_freq):
                remote, local, mine, other = descriptor(b, w, h)
                pl.when(other)(remote.wait_send)
        if half_way < per_granule:
            for h in range(n_freq):
                copy, used = detour(b, h)
                pl.when(used)(copy.wait_send)
        return 0

    lax.fori_loop(0, chunks, drain, 0)
    for slot in range(per_granule - half_way):
        copy, used = onward(slot)
        pl.when(used)(copy.wait_send)
    for part in range(per_granule):
        for sx in range(n_seg):
            pl.when(along_used(sx, part))(along(sx, part).wait_send)
            for w in range(1, n_seg + 1):
                for tx in range(n_seg):
                    pl.when(hub_target(sx, w, tx))(across(sx, w, tx, part).wait_send)


def shards(samples, live):
    ch_dev, segs, length = samples.shape
    n_chan, n_seg, n_freq = (lax.axis_size(a) for a in ("chan", "seg", "freq"))
    owned = ch_dev // n_seg
    half = BINS // n_freq
    core_ch = ch_dev // n_freq
    chunks = core_ch // CHUNK_CH
    chunk_rows = CHUNK_CH * segs
    quarter = length // QUARTERS
    window = (n_seg + 1) * owned
    result = pl.pallas_call(
        functools.partial(kernel, n_chan, n_seg, n_freq),
        out_shape=jax.ShapeDtypeStruct((owned, 2 * OFFSETS, half), jnp.bfloat16),
        in_specs=[pl.BlockSpec(memory_space=pltpu.HBM)] * 2,
        out_specs=pl.BlockSpec(memory_space=pltpu.VMEM),
        scratch_shapes=[
            pltpu.VMEM(live.shape[::-1], jnp.int32),
            pltpu.VMEM(live.shape, jnp.float32),
            pltpu.VMEM((chunks, QUARTERS * chunk_rows, quarter), jnp.bfloat16),
            pltpu.VMEM((quarter, 2 * BINS), jnp.bfloat16),
            pltpu.VMEM((2, quarter // FINE, BINS), jnp.float32),
            pltpu.VMEM((n_freq, core_ch * segs, 2 * half), jnp.bfloat16),
            pltpu.VMEM((n_seg, n_seg + 1, owned * segs, 2 * half), jnp.bfloat16),
            pltpu.VMEM((window, n_seg * segs, 2 * half), jnp.bfloat16),
            pltpu.VMEM((window, n_seg * segs), jnp.float32),
            pltpu.VMEM((owned, 2 * OFFSETS, half), jnp.float32),
            pltpu.SemaphoreType.DMA,
            pltpu.SemaphoreType.DMA((chunks, QUARTERS)),
            pltpu.SemaphoreType.DMA((chunks, n_seg + 1, n_freq)),
            pltpu.SemaphoreType.DMA((n_seg, n_seg + 1, owned // CHUNK_CH)),
            pltpu.SemaphoreType.DMA((n_seg, owned // CHUNK_CH)),
            pltpu.SemaphoreType.DMA((n_seg, n_seg, n_seg, owned // CHUNK_CH)),
            pltpu.VMEM((owned // CHUNK_CH, chunk_rows, 2 * half), jnp.bfloat16),
            pltpu.SemaphoreType.DMA((owned // CHUNK_CH,)),
            pltpu.SemaphoreType.DMA((owned // CHUNK_CH,)),
        ],
        compiler_params=pltpu.CompilerParams(
            collective_id=0, has_side_effects=True, vmem_limit_bytes=48 * 1024 * 1024
        ),
    )(samples.reshape(ch_dev * segs, length), live.T)
    return result.reshape(owned, OFFSETS, 2, half)


def solution(mesh):
    return jax.shard_map(
        shards,
        mesh=mesh,
        in_specs=(P(("cable", "chan"), "seg", None), P("cable", None)),
        out_specs=P(("cable", "chan", "seg"), None, None, "freq"),
        check_vma=False,
    )
```

profile of v0, /device:TPU:1, one launch (start us, length us, event | category | flops | bytes accessed | tf_op | source)
XLA Modules:
  0.0 22.0 jit_solution(16651438880193795299)
XLA Ops:
  0.0 0.0 copy-start
  0.0 0.7 %copy-done = s32[256,16]{0,1:T(8,128)S(1)} copy-done((s32[256,16]{0,1:T(8,128)S(1)}, s32[256,16]{0,1:T(8,128)}, u32[]{:S(2)}) %copy-start) | copy-done | bytes 16408
  0.7 20.3 %shard_map.28 = bf16[32,128,128]{2,1,0:T(8,128)(2,1)S(1)} custom-call(bf16[512,8192]{1,0:T(8,128)(2,1)} %bitcast.5, s32[16,256]{1,0:T(8,128)S(1)} %bitcast.4), custom_call_target="tpu_custom_call" | custom-call | tf_op jit(solution)/shard_map/pallas_call | solution.py:361
  21.0 1.0 %copy.4 = bf16[32,64,2,128]{3,2,1,0:T(2,128)(2,1)} copy(bf16[32,64,2,128]{3,2,1,0:T(2,128)(2,1)S(1)} %bitcast.3) | data formatting | bytes 2097152
Async XLA Ops:
  0.0 0.7 %copy-start = (s32[256,16]{0,1:T(8,128)S(1)}, s32[256,16]{0,1:T(8,128)}, u32[]{:S(2)}) copy-start(s32[256,16]{0,1:T(8,128)} %param.3) | copy-start | bytes 49156
where the time goes:
time: 22.2 us; the launch traced here: 22 us
  Pallas kernels  20.3 us (91%)
  local copies, waits for them, and re-layouts  1.69 us (8%)
    pallas_call x1, Pallas kernels, shards(): pl.pallas_call(functools.partial(kernel, n_chan, n_seg, n_freq), out_shap...  20.3 us
    unnamed x3, local copies, waits for them, and re-layouts  1.69 us

commit v1 on v0

--- a/solution.py
+++ b/solution.py
@@ -273,9 +273,8 @@
     span = n_seg * segs
     row_id = lax.broadcasted_iota(jnp.int32, (2 * KB, KB * span), 0)
     col_id = lax.broadcasted_iota(jnp.int32, (2 * KB, KB * span), 1) // span
-    hit = row_id // 2 == col_id
-    sum_re = jnp.where(jnp.logical_and(hit, row_id % 2 == 0), 1.0, 0.0).astype(jnp.bfloat16)
-    sum_im = jnp.where(jnp.logical_and(hit, row_id % 2 == 1), 1.0, 0.0).astype(jnp.bfloat16)
+    sum_rows = jnp.where(row_id // 2 == col_id, 1.0, 0.0).astype(jnp.bfloat16)
+    real_row = lax.broadcasted_iota(jnp.int32, (2 * KB, half), 0) % 2 == 0
 
     sub_parts = KB // CHUNK_CH
     for t in range((n_seg + 1) * owned // KB):
@@ -315,9 +314,9 @@
             other_re, other_im = other[:, :, :half], other[:, :, half:]
             re = own_re * other_re + own_im * other_im
             im = own_re * other_im - own_im * other_re
-            total = jnp.dot(
-                sum_re, re.reshape(KB * span, half), preferred_element_type=jnp.float32
-            ) + jnp.dot(sum_im, im.reshape(KB * span, half), preferred_element_type=jnp.float32)
+            both = jnp.concatenate([re, im], axis=2).reshape(KB * span, 2 * half)
+            total = jnp.dot(sum_rows, both, preferred_element_type=jnp.float32)
+            total = jnp.where(real_row, total[:, :half], total[:, half:])
             rows = pl.ds(pl.multiple_of(2 * KB * kb, 2 * KB), 2 * KB)
             out[i, rows, :] = (total * inv[i, rows, :]).astype(jnp.bfloat16)
             return 0

time: 22.2 us -> 21.3 us (0.959)
  Pallas kernels: 20.3 us -> 19.4 us
    pallas_call x1, Pallas kernels: 20.3 us -> 19.4 us  [shards(): pl.pallas_call(functools.partial(kernel, n_chan, n_seg, n_freq), out_shap...]
where the time goes in v1:
time: 21.3 us; the launch traced here: 21.1 us
  Pallas kernels  19.4 us (91%)
  local copies, waits for them, and re-layouts  1.69 us (8%)
    pallas_call x1, Pallas kernels, shards(): pl.pallas_call(functools.partial(kernel, n_chan, n_seg, n_freq), out_shap...  19.4 us
    unnamed x3, local copies, waits for them, and re-layouts  1.69 us

profile of v1, /device:TPU:1, one launch (start us, length us, event | category | flops | bytes accessed | tf_op | source)
XLA Modules:
  0.0 21.1 jit_solution(17711563777923502653)
XLA Ops:
  0.0 0.0 copy-start
  0.0 0.7 %copy-done = s32[256,16]{0,1:T(8,128)S(1)} copy-done((s32[256,16]{0,1:T(8,128)S(1)}, s32[256,16]{0,1:T(8,128)}, u32[]{:S(2)}) %copy-start) | copy-done | bytes 16408
  0.7 19.4 %shard_map.28 = bf16[32,128,128]{2,1,0:T(8,128)(2,1)S(1)} custom-call(bf16[512,8192]{1,0:T(8,128)(2,1)} %bitcast.5, s32[16,256]{1,0:T(8,128)S(1)} %bitcast.4), custom_call_target="tpu_custom_call" | custom-call | tf_op jit(solution)/shard_map/pallas_call | solution.py:360
  20.1 1.0 %copy.4 = bf16[32,64,2,128]{3,2,1,0:T(2,128)(2,1)} copy(bf16[32,64,2,128]{3,2,1,0:T(2,128)(2,1)S(1)} %bitcast.3) | data formatting | bytes 2097152
Async XLA Ops:
  0.0 0.7 %copy-start = (s32[256,16]{0,1:T(8,128)S(1)}, s32[256,16]{0,1:T(8,128)}, u32[]{:S(2)}) copy-start(s32[256,16]{0,1:T(8,128)} %param.3) | copy-start | bytes 49156

commit v2 on v1

--- a/solution.py
+++ b/solution.py
@@ -186,6 +186,17 @@
     alpha = jnp.where(phase == 0, 1.0, jnp.where(phase == 2, -1.0, 0.0))
     beta = jnp.where(phase == 1, 1.0, jnp.where(phase == 3, -1.0, 0.0))
     sigma = jnp.where(lane_k % 2 == 0, 1.0, -1.0)
+
+    def send_late(b):
+        later = c * gpc + b // per_granule > 0
+        for w in range(n_seg, 0, -1):
+            for h in range(n_freq):
+                remote, local, mine, other = descriptor(b, w, h)
+                pl.when(jnp.logical_and(other, later))(remote.start)
+        if half_way < per_granule:
+            for h in range(n_freq):
+                copy, used = detour(b, h)
+                pl.when(used)(copy.start)
 
     def transform(b, _):
         for q in range(QUARTERS):
@@ -212,18 +223,18 @@
         for h in range(n_freq):
             snd[h, rows, :half] = white_re[:, h * half : (h + 1) * half]
             snd[h, rows, half:] = white_im[:, h * half : (h + 1) * half]
+        first_granule = c * gpc + b // per_granule == 0
         for w in range(n_seg, -1, -1):
             for h in range(n_freq):
                 remote, local, mine, other = descriptor(b, w, h)
-                pl.when(other)(remote.start)
+                soon = other if w == 0 else jnp.logical_and(other, first_granule)
+                pl.when(soon)(remote.start)
                 pl.when(mine)(local.start)
-        if half_way < per_granule:
-            for h in range(n_freq):
-                copy, used = detour(b, h)
-                pl.when(used)(copy.start)
+        pl.when(b > 0)(functools.partial(send_late, b - 1))
         return 0
 
     lax.fori_loop(0, chunks, transform, 0)
+    send_late(jnp.int32(chunks - 1))
 
     last_block = chans // owned - 1
     for w in range(n_seg + 1):

time: 21.3 us -> 22 us (1.033)
  Pallas kernels: 19.4 us -> 20.1 us
    pallas_call x1, Pallas kernels: 19.4 us -> 20.1 us  [shards(): pl.pallas_call(functools.partial(kernel, n_chan, n_seg, n_freq), out_shap...]
where the time goes in v2:
time: 22 us; the launch traced here: 21.8 us
  Pallas kernels  20.1 us (91%)
  local copies, waits for them, and re-layouts  1.69 us (8%)
    pallas_call x1, Pallas kernels, shards(): pl.pallas_call(functools.partial(kernel, n_chan, n_seg, n_freq), out_shap...  20.1 us
    unnamed x3, local copies, waits for them, and re-layouts  1.69 us

profile of v2, /device:TPU:1, one launch (start us, length us, event | category | flops | bytes accessed | tf_op | source)
XLA Modules:
  0.0 21.8 jit_solution(14955285673769047311)
XLA Ops:
  0.0 0.0 copy-start
  0.0 0.7 %copy-done = s32[256,16]{0,1:T(8,128)S(1)} copy-done((s32[256,16]{0,1:T(8,128)S(1)}, s32[256,16]{0,1:T(8,128)}, u32[]{:S(2)}) %copy-start) | copy-done | bytes 16408
  0.7 20.1 %shard_map.28 = bf16[32,128,128]{2,1,0:T(8,128)(2,1)S(1)} custom-call(bf16[512,8192]{1,0:T(8,128)(2,1)} %bitcast.5, s32[16,256]{1,0:T(8,128)S(1)} %bitcast.4), custom_call_target="tpu_custom_call" | custom-call | tf_op jit(solution)/shard_map/pallas_call | solution.py:371
  20.8 1.0 %copy.4 = bf16[32,64,2,128]{3,2,1,0:T(2,128)(2,1)} copy(bf16[32,64,2,128]{3,2,1,0:T(2,128)(2,1)S(1)} %bitcast.3) | data formatting | bytes 2097152
Async XLA Ops:
  0.0 0.7 %copy-start = (s32[256,16]{0,1:T(8,128)S(1)}, s32[256,16]{0,1:T(8,128)}, u32[]{:S(2)}) copy-start(s32[256,16]{0,1:T(8,128)} %param.3) | copy-start | bytes 49156

commit v3 on v2

--- a/solution.py
+++ b/solution.py
@@ -188,10 +188,11 @@
     sigma = jnp.where(lane_k % 2 == 0, 1.0, -1.0)
 
     def send_late(b):
-        later = c * gpc + b // per_granule > 0
+        granule = c * gpc + b // per_granule
         for w in range(n_seg, 0, -1):
             for h in range(n_freq):
                 remote, local, mine, other = descriptor(b, w, h)
+                later = jnp.logical_and(granule > 0, granule < w)
                 pl.when(jnp.logical_and(other, later))(remote.start)
         if half_way < per_granule:
             for h in range(n_freq):
@@ -223,11 +224,12 @@
         for h in range(n_freq):
             snd[h, rows, :half] = white_re[:, h * half : (h + 1) * half]
             snd[h, rows, half:] = white_im[:, h * half : (h + 1) * half]
-        first_granule = c * gpc + b // per_granule == 0
+        granule = c * gpc + b // per_granule
         for w in range(n_seg, -1, -1):
             for h in range(n_freq):
                 remote, local, mine, other = descriptor(b, w, h)
-                soon = other if w == 0 else jnp.logical_and(other, first_granule)
+                at_once = jnp.logical_or(granule == 0, granule >= w)
+                soon = jnp.logical_and(other, at_once)
                 pl.when(soon)(remote.start)
                 pl.when(mine)(local.start)
         pl.when(b > 0)(functools.partial(send_late, b - 1))

time: 22 us -> 22 us (level)
  no operation moved by 1% of the time
where the time goes in v3:
time: 22 us; the launch traced here: 21.8 us
  Pallas kernels  20.1 us (91%)
  local copies, waits for them, and re-layouts  1.69 us (8%)
    pallas_call x1, Pallas kernels, shards(): pl.pallas_call(functools.partial(kernel, n_chan, n_seg, n_freq), out_shap...  20.1 us
    unnamed x3, local copies, waits for them, and re-layouts  1.69 us

profile of v3, /device:TPU:1, one launch (start us, length us, event | category | flops | bytes accessed | tf_op | source)
XLA Modules:
  0.0 21.8 jit_solution(3244932642990019218)
XLA Ops:
  0.0 0.0 copy-start
  0.0 0.7 %copy-done = s32[256,16]{0,1:T(8,128)S(1)} copy-done((s32[256,16]{0,1:T(8,128)S(1)}, s32[256,16]{0,1:T(8,128)}, u32[]{:S(2)}) %copy-start) | copy-done | bytes 16408
  0.7 20.1 %shard_map.28 = bf16[32,128,128]{2,1,0:T(8,128)(2,1)S(1)} custom-call(bf16[512,8192]{1,0:T(8,128)(2,1)} %bitcast.5, s32[16,256]{1,0:T(8,128)S(1)} %bitcast.4), custom_call_target="tpu_custom_call" | custom-call | tf_op jit(solution)/shard_map/pallas_call | solution.py:373
  20.8 1.0 %copy.4 = bf16[32,64,2,128]{3,2,1,0:T(2,128)(2,1)} copy(bf16[32,64,2,128]{3,2,1,0:T(2,128)(2,1)S(1)} %bitcast.3) | data formatting | bytes 2097152
Async XLA Ops:
  0.0 0.7 %copy-start = (s32[256,16]{0,1:T(8,128)S(1)}, s32[256,16]{0,1:T(8,128)}, u32[]{:S(2)}) copy-start(s32[256,16]{0,1:T(8,128)} %param.3) | copy-start | bytes 49156
